TPU v7x, 128 devices: a whole 4x4x4 slice. The times are simulated.
128 devices in a mesh: outer: 4 (over x_hi, core), inner: 32 (over z, x_lo, y).
Axes of the slice: x: 4 (x_hi: 2, x_lo: 2; x = x_hi * 2 + x_lo), y: 4, z: 4, core: 2. Of those that a mesh axis runs over, the one named last changes fastest.
Arguments:
- coeffs: bfloat16 [32, 8, 131072], P(None, None, ('outer', 'inner')), may hold values from -6 to 6
- source_mats: bfloat16 [2, 2, 32, 32, 131072], P(None, None, None, None, ('outer', 'inner')), may hold values from -0.75 to 0.75
- middle_mats: bfloat16 [32, 32, 131072], P(None, None, ('outer', 'inner')), may hold values from -1 to 1
- target_mats: bfloat16 [2, 2, 32, 32, 131072], P(None, None, None, None, ('outer', 'inner')), may hold values from -0.75 to 0.75
Outputs:
- target_coeffs: bfloat16 [32, 8, 131072], P(None, None, ('outer', 'inner'))
All inputs are finite; a program needn't handle non-finite values.
Results may differ from a plain program's by a relative error of at most 0.0071.
Values may be sent and summed in bfloat16 or wider, within the bound.
A program may use at most 192 MiB of HBM per device.

v0:
```python
import jax
import jax.numpy as jnp
from jax import lax
from jax.experimental import pallas as pl
from jax.experimental.pallas import tpu as pltpu
from jax.sharding import PartitionSpec as P

F32 = jnp.float32
BF16 = jnp.bfloat16
MESH = pl.DeviceIdType.MESH
TILES = 8
EARLY = 4
LAGS = (0, 0, 4, 6, 8, 9, 10)
PAIRS = 4
TILE = (16, 16, 128)


def flip1(v):
    return v + 1 - 2 * lax.rem(v, 2)


def flip(v, k):
    total = 0
    for bit in (1, 2, 4):
        total = total + bit * lax.rem(lax.div(v, bit) + lax.div(k, bit), 2)
    return total


def lane_blocks(v):
    lane = lax.broadcasted_iota(jnp.int32, (16, 128), 1)
    low = lane < 64
    even = (lane & 32) == 0
    s = [None] * 4
    for a in range(2):
        s[a] = jnp.where(low, v[a], pltpu.roll(v[a + 2], 64, 1))
        s[a + 2] = jnp.where(low, pltpu.roll(v[a], 64, 1), v[a + 2])
    out = [None] * 4
    for a in (0, 2):
        out[a] = jnp.where(even, s[a], pltpu.roll(s[a + 1], 32, 1))
        out[a + 1] = jnp.where(even, pltpu.roll(s[a], 96, 1), s[a + 1])
    return out


def level(mats, xf, mf, emit, part=None):
    n = len(mats)

    def widen(g, slot):
        for s in range(n):
            mf[slot, s] = mats[s](g * 4).astype(F32)

    widen(0, 0)

    def body(h, _):
        for slot in range(2):
            g = h * 2 + slot
            widen(lax.rem(g + 1, 8), 1 - slot)
            acc = [None if part is None else part[g * 4 + i] for i in range(4)]
            for s in range(n):
                for j in range(32):
                    x = xf[s, j]
                    for i in range(4):
                        v = x * mf[slot, s, i, j : j + 1, :]
                        acc[i] = v if acc[i] is None else acc[i] + v
            emit(g * 4, acc)
        return 0

    lax.fori_loop(0, 4, body, 0)


def kernel(
    coeffs, source, middle, target, out,
    ms, mm, mt, c0, x1, x1p, snd, rcv, pk, un, x4, x4p, res, xf, mf, part, fin,
    m_sem, c_sem, cs_sem, cr_sem, xs_sem, xr_sem, as_sem, ar_sem, al_sem,
    ys_sem, yr_sem, yl_sem, ts_sem, tr_sem, o_sem,
):
    outer, inner = lax.axis_index("outer"), lax.axis_index("inner")
    own, y = lax.div(inner, 4), lax.rem(inner, 4)
    core_dev = (flip1(outer), inner)
    far_dev = (lax.rem(outer + 2, 4), inner)

    def ring_dev(k):
        return (outer, flip(own, k) * 4 + y)

    def y_dev(d):
        return (outer, own * 4 + flip(y, d))

    def tile(k):
        return flip(own, k)

    def lanes(k):
        return pl.ds(pl.multiple_of(tile(k) * 128, 128), 128)

    def pair(q):
        return flip(lax.div(own, 2), q)

    def pair_lanes(q):
        return pl.ds(pl.multiple_of(pair(q) * 256, 256), 256)

    def pair_rows(q):
        return pl.ds(pl.multiple_of(pair(q) * 16, 16), 16)

    def mat_copy(stage, q):
        r = pair_lanes(q)
        if stage < 4:
            at = (stage // 2, stage % 2, slice(None), slice(None), r)
            ends = (source.at[at], ms.at[at])
        elif stage == 4:
            ends = (middle.at[:, :, r], mm.at[:, :, r])
        else:
            at = ((stage - 5) // 2, (stage - 5) % 2, slice(None), slice(None), r)
            ends = (target.at[at], mt.at[at])
        return pltpu.make_async_copy(*ends, m_sem.at[stage, q])

    def coeff_copy(q):
        return pltpu.make_async_copy(coeffs.at[:, pair_rows(q)], c0.at[0, :, pair_rows(q)], c_sem.at[q])

    def remote(src, dst, send, recv, device):
        return pltpu.make_async_remote_copy(
            src_ref=src, dst_ref=dst, send_sem=send, recv_sem=recv, device_id=device, device_id_type=MESH
        )

    def coeff_send(q):
        return remote(coeffs.at[:, pair_rows(q)], c0.at[1, :, pair_rows(q)], cs_sem.at[q], cr_sem.at[q], core_dev)

    def far_send(k):
        return remote(x1.at[k], x1p.at[k], xs_sem.at[k], xr_sem.at[k], far_dev)

    def swap_send(k):
        return remote(snd.at[k], rcv.at[k], as_sem.at[k], ar_sem.at[k], ring_dev(k))

    def swap_local():
        return pltpu.make_async_copy(snd.at[0], rcv.at[0], al_sem)

    def y_send(k, d):
        return remote(
            pk.at[k, lax.div(flip(y, d), 2)], un.at[k, y], ys_sem.at[k, d], yr_sem.at[k, d], y_dev(d)
        )

    def y_arrival(k, d):
        return remote(
            pk.at[k, lax.div(flip(y, d), 2)], un.at[k, flip(y, d)], ys_sem.at[k, d], yr_sem.at[k, d], y_dev(d)
        )

    def y_local(k):
        return pltpu.make_async_copy(pk.at[k, lax.div(y, 2)], un.at[k, y], yl_sem.at[k])

    def last_send(k):
        return remote(x4.at[k], x4p.at[k], ts_sem.at[k], tr_sem.at[k], y_dev(2))

    def out_copy(q):
        return pltpu.make_async_copy(res.at[:, pair_rows(q)], out.at[:, pair_rows(q)], o_sem.at[q])

    def each(count, fn):
        def body(k, _):
            fn(k)
            return 0

        lax.fori_loop(0, count, body, 0)

    barrier = pltpu.get_barrier_semaphore()
    peers = [core_dev, far_dev] + [y_dev(d) for d in (1, 2, 3)] + [ring_dev(k) for k in range(1, 8)]
    for peer in peers:
        pl.semaphore_signal(barrier, inc=1, device_id=peer, device_id_type=MESH)

    def start_pair(q):
        coeff_copy(q).start()
        mat_copy(0, q).start()

    each(PAIRS, start_pair)
    for stage in range(1, 9):
        each(PAIRS, lambda q, stage=stage: mat_copy(stage, q).start())

    def await_pair(k, *waits):
        @pl.when(lax.rem(k, 2) == 0)
        def _():
            for wait in waits:
                wait(lax.div(k, 2))

    def mats(ref, lead, k):
        ln = lanes(k)
        return [lambda i, at=at: ref[(*at, pl.ds(i, 4), slice(None), ln)] for at in lead]

    def fill(s, ref):
        for h in range(16):
            v = ref[h].astype(F32)
            xf[s, 2 * h] = v[:8]
            xf[s, 2 * h + 1] = v[8:]

    def emit_to(ref):
        def emit(i, acc):
            h = lax.div(i, 2)
            for a in range(2):
                ref[h + a] = jnp.concatenate(acc[2 * a : 2 * a + 2], 0).astype(BF16)

        return emit

    def keep(ref):
        def emit(i, acc):
            for a in range(4):
                ref[i + a] = acc[a]

        return emit

    def first_fill(s, k):
        upper = lax.rem(tile(k), 2) == 1
        rows = pair_rows(lax.div(k, 2))
        for j in range(32):
            v = c0[s, j, rows, :].astype(F32)
            xf[0, j] = jnp.where(upper, v[8:], v[:8])

    def first_own(k):
        await_pair(k, lambda q: coeff_copy(q).wait(), lambda q: mat_copy(0, q).wait())
        first_fill(0, k)
        level(mats(ms, ((0, 0),), k), xf, mf, keep(part.at[k]))

    def first_level(k):
        await_pair(k, lambda q: coeff_send(q).wait_recv(), lambda q: mat_copy(1, q).wait())
        first_fill(1, k)
        level(mats(ms, ((0, 1),), k), xf, mf, emit_to(x1.at[k]), part.at[k])
        far_send(k).start()

    def second_own(k):
        await_pair(k, lambda q: mat_copy(2, q).wait())
        fill(0, x1.at[k])
        level(mats(ms, ((1, 0),), k), xf, mf, keep(part.at[k]))

    def second_level(k):
        await_pair(k, lambda q: mat_copy(3, q).wait(), lambda q: mat_copy(4, q).wait())
        far_send(k).wait_recv()
        fill(0, x1p.at[k])

        def emit(i, acc):
            for a in range(4):
                xf[1, i + a] = acc[a].astype(BF16).astype(F32)

        level(mats(ms, ((1, 1),), k), xf, mf, emit, part.at[k])
        level(mats(mm, ((),), k), xf.at[1:2], mf, emit_to(snd.at[k]))

        @pl.when(k == 0)
        def _():
            swap_local().start()

        @pl.when(k > 0)
        def _():
            swap_send(k).start()

    def regroup(k):
        @pl.when(k == 0)
        def _():
            swap_local().wait()

        @pl.when(k > 0)
        def _():
            swap_send(k).wait_recv()

        for a in range(4):
            v = lane_blocks([rcv[k, a * 4 + c].astype(F32) for c in range(4)])
            for b in range(4):
                pk[k, b // 2, b % 2, a] = v[b].astype(BF16)
        for d in (1, 2, 3):
            y_send(k, d).start()
        y_local(k).start()

    def third_level(k):
        await_pair(k, lambda q: mat_copy(5, q).wait(), lambda q: mat_copy(6, q).wait())
        y_local(k).wait()
        for d in (1, 2, 3):
            y_arrival(k, d).wait_recv()
        for s in range(2):
            which = lax.rem(y, 2) if s == 0 else 1 - lax.rem(y, 2)
            for a in range(4):
                v = lane_blocks([un[k, b, which, a].astype(F32) for b in range(4)])
                for c in range(4):
                    xf[s, a * 8 + c * 2] = v[c][:8]
                    xf[s, a * 8 + c * 2 + 1] = v[c][8:]
        level(mats(mt, ((0, 0), (0, 1)), k), xf, mf, emit_to(x4.at[k]))
        last_send(k).start()

    def fourth_own(k):
        await_pair(k, lambda q: mat_copy(7, q).wait())
        fill(0, x4.at[k])
        level(mats(mt, ((1, 0),), k), xf, mf, keep(part.at[k]))

    def fourth_level(k):
        await_pair(k, lambda q: mat_copy(8, q).wait())
        last_send(k).wait_recv()
        fill(0, x4p.at[k])
        half = lax.rem(tile(k), 2)
        level(mats(mt, ((1, 1),), k), xf, mf, keep(fin.at[half]), part.at[k])

        @pl.when(lax.rem(k, 2) == 1)
        def _():
            q = lax.div(k, 2)
            rows = pair_rows(q)
            for i in range(32):
                res[i, rows, :] = jnp.concatenate([fin[0, i], fin[1, i]], 0).astype(BF16)
            out_copy(q).start()

    def early(k, _):
        first_own(k)
        return 0

    lax.fori_loop(0, EARLY, early, 0)
    pl.semaphore_wait(barrier, len(peers))
    each(PAIRS, lambda q: coeff_send(q).start())
    lax.fori_loop(EARLY, TILES, early, 0)

    stages = tuple(zip(LAGS, (first_level, second_own, second_level, regroup, third_level, fourth_own, fourth_level)))

    def step(n, _):
        for late, stage in stages:

            @pl.when(jnp.logical_and(n >= late, n < TILES + late))
            def _(late=late, stage=stage):
                stage(n - late)

        return 0

    lax.fori_loop(0, TILES + stages[-1][0], step, 0)

    def finish(k):
        far_send(k).wait_send()
        for d in (1, 2, 3):
            y_send(k, d).wait_send()
        last_send(k).wait_send()

        @pl.when(k > 0)
        def _():
            swap_send(k).wait_send()

    def finish_pair(q):
        coeff_send(q).wait_send()
        out_copy(q).wait()

    each(TILES, finish)
    each(PAIRS, finish_pair)


def per_device(coeffs, source_mats, middle_mats, target_mats):
    hbm = pl.BlockSpec(memory_space=pl.ANY)
    vm = lambda *s: pltpu.VMEM(s, BF16)
    dma = lambda *s: pltpu.SemaphoreType.DMA(s)
    out = pl.pallas_call(
        kernel,
        out_shape=jax.ShapeDtypeStruct((32, 64, 128), BF16),
        in_specs=[hbm] * 4,
        out_specs=hbm,
        scratch_shapes=[
            vm(2, 2, 32, 32, 1024),
            vm(32, 32, 1024),
            vm(2, 2, 32, 32, 1024),
            vm(2, 32, 64, 128),
            vm(8, *TILE),
            vm(8, *TILE),
            vm(8, *TILE),
            vm(8, *TILE),
            vm(8, 2, 2, 4, 16, 128),
            vm(8, 4, 2, 4, 16, 128),
            vm(8, *TILE),
            vm(8, *TILE),
            vm(32, 64, 128),
            pltpu.VMEM((2, 32, 8, 128), F32),
            pltpu.VMEM((2, 2, 4, 32, 128), F32),
            pltpu.VMEM((8, 32, 8, 128), F32),
            pltpu.VMEM((2, 32, 8, 128), F32),
            dma(9, 4), dma(4), dma(4), dma(4), dma(8), dma(8), dma(8), dma(8),
            pltpu.SemaphoreType.DMA,
            dma(8, 4), dma(8, 4), dma(8), dma(8), dma(8), dma(4),
        ],
        compiler_params=pltpu.CompilerParams(
            collective_id=0, has_side_effects=True, vmem_limit_bytes=60 << 20
        ),
        name="butterfly",
    )(
        coeffs.reshape(32, 8, 8, 128).swapaxes(1, 2).reshape(32, 64, 128),
        source_mats,
        middle_mats,
        target_mats,
    )
    return out.reshape(32, 8, 8, 128).swapaxes(1, 2).reshape(32, 8, 1024)


def solution(mesh):
    return jax.shard_map(
        per_device,
        mesh=mesh,
        in_specs=(
            P(None, None, ("outer", "inner")),
            P(None, None, None, None, ("outer", "inner")),
            P(None, None, ("outer", "inner")),
            P(None, None, None, None, ("outer", "inner")),
        ),
        out_specs=P(None, None, ("outer", "inner")),
        check_vma=False,
    )
```

profile of v0, /device:TPU:0, one launch (start us, length us, event | category | flops | bytes accessed | tf_op | source)
XLA Modules:
  0.0 49.2 jit_solution(12577462353963202285)
XLA Ops:
  0.0 47.3 %butterfly.1 = bf16[32,64,128]{2,1,0:T(8,128)(2,1)} custom-call(bf16[32,64,128]{2,1,0:T(8,128)(2,1)} %bitcast.11, bf16[2,2,32,32,1024]{4,3,2,1,0:T(8,128)(2,1)} %source.1, bf16[32,32,1024]{2,1,0:T(8,128)(2,1)} %middle.1, bf16[2,2,32,32,1024]{4,3,2,1,0:T(8,128)(2,1)} %target.1), custom_call_target="tpu_custom_call" | custom-call | tf_op jit(solution)/shard_map/butterfly/pallas_call | solution.py:343
  47.3 1.9 %copy.6 = bf16[32,8,1024]{2,1,0:T(8,128)(2,1)} copy(bf16[32,8,1024]{2,1,0:T(8,128)(2,1)} %bitcast.10) | data formatting | bytes 1048576
where the time goes:
time: 49.4 us; the launch traced here: 49.2 us
  Pallas kernels  47.3 us (96%)
  local copies, waits for them, and re-layouts  1.87 us (4%)
    pallas_call x1, Pallas kernels, per_device(): pl.pallas_call(kernel, out_shape=jax.ShapeDtypeStruct((32, 64, 128), BF16...  47.3 us
    unnamed x1, local copies, waits for them, and re-layouts  1.87 us

commit v1 on v0

--- a/solution.py
+++ b/solution.py
@@ -10,7 +10,7 @@
 MESH = pl.DeviceIdType.MESH
 TILES = 8
 EARLY = 4
-LAGS = (0, 0, 4, 6, 8, 9, 10)
+LAGS = (0, 0, 3, 5, 7, 8, 9)
 PAIRS = 4
 TILE = (16, 16, 128)
 
@@ -41,7 +41,7 @@
     return out
 
 
-def level(mats, xf, mf, emit, part=None):
+def level(mats, xf, mf, emit, part=None, halfway=None):
     n = len(mats)
 
     def widen(g, slot):
@@ -62,6 +62,8 @@
                         v = x * mf[slot, s, i, j : j + 1, :]
                         acc[i] = v if acc[i] is None else acc[i] + v
             emit(g * 4, acc)
+        if halfway is not None:
+            pl.when(h == 1)(halfway)
         return 0
 
     lax.fori_loop(0, 4, body, 0)
@@ -122,11 +124,16 @@
     def coeff_send(q):
         return remote(coeffs.at[:, pair_rows(q)], c0.at[1, :, pair_rows(q)], cs_sem.at[q], cr_sem.at[q], core_dev)
 
-    def far_send(k):
-        return remote(x1.at[k], x1p.at[k], xs_sem.at[k], xr_sem.at[k], far_dev)
-
-    def swap_send(k):
-        return remote(snd.at[k], rcv.at[k], as_sem.at[k], ar_sem.at[k], ring_dev(k))
+    def part_of(k, u):
+        return (k, pl.ds(u * 8, 8))
+
+    def far_send(k, u):
+        at = part_of(k, u)
+        return remote(x1.at[at], x1p.at[at], xs_sem.at[k, u], xr_sem.at[k, u], far_dev)
+
+    def swap_send(k, u):
+        at = part_of(k, u)
+        return remote(snd.at[at], rcv.at[at], as_sem.at[k, u], ar_sem.at[k, u], ring_dev(k))
 
     def swap_local():
         return pltpu.make_async_copy(snd.at[0], rcv.at[0], al_sem)
@@ -144,8 +151,9 @@
     def y_local(k):
         return pltpu.make_async_copy(pk.at[k, lax.div(y, 2)], un.at[k, y], yl_sem.at[k])
 
-    def last_send(k):
-        return remote(x4.at[k], x4p.at[k], ts_sem.at[k], tr_sem.at[k], y_dev(2))
+    def last_send(k, u):
+        at = part_of(k, u)
+        return remote(x4.at[at], x4p.at[at], ts_sem.at[k, u], tr_sem.at[k, u], y_dev(2))
 
     def out_copy(q):
         return pltpu.make_async_copy(res.at[:, pair_rows(q)], out.at[:, pair_rows(q)], o_sem.at[q])
@@ -216,8 +224,8 @@
     def first_level(k):
         await_pair(k, lambda q: coeff_send(q).wait_recv(), lambda q: mat_copy(1, q).wait())
         first_fill(1, k)
-        level(mats(ms, ((0, 1),), k), xf, mf, emit_to(x1.at[k]), part.at[k])
-        far_send(k).start()
+        level(mats(ms, ((0, 1),), k), xf, mf, emit_to(x1.at[k]), part.at[k], lambda: far_send(k, 0).start())
+        far_send(k, 1).start()
 
     def second_own(k):
         await_pair(k, lambda q: mat_copy(2, q).wait())
@@ -226,7 +234,8 @@
 
     def second_level(k):
         await_pair(k, lambda q: mat_copy(3, q).wait(), lambda q: mat_copy(4, q).wait())
-        far_send(k).wait_recv()
+        far_send(k, 0).wait_recv()
+        far_send(k, 1).wait_recv()
         fill(0, x1p.at[k])
 
         def emit(i, acc):
@@ -234,7 +243,12 @@
                 xf[1, i + a] = acc[a].astype(BF16).astype(F32)
 
         level(mats(ms, ((1, 1),), k), xf, mf, emit, part.at[k])
-        level(mats(mm, ((),), k), xf.at[1:2], mf, emit_to(snd.at[k]))
+        def halfway():
+            @pl.when(k > 0)
+            def _():
+                swap_send(k, 0).start()
+
+        level(mats(mm, ((),), k), xf.at[1:2], mf, emit_to(snd.at[k]), None, halfway)
 
         @pl.when(k == 0)
         def _():
@@ -242,7 +256,7 @@
 
         @pl.when(k > 0)
         def _():
-            swap_send(k).start()
+            swap_send(k, 1).start()
 
     def regroup(k):
         @pl.when(k == 0)
@@ -251,7 +265,8 @@
 
         @pl.when(k > 0)
         def _():
-            swap_send(k).wait_recv()
+            swap_send(k, 0).wait_recv()
+            swap_send(k, 1).wait_recv()
 
         for a in range(4):
             v = lane_blocks([rcv[k, a * 4 + c].astype(F32) for c in range(4)])
@@ -273,8 +288,8 @@
                 for c in range(4):
                     xf[s, a * 8 + c * 2] = v[c][:8]
                     xf[s, a * 8 + c * 2 + 1] = v[c][8:]
-        level(mats(mt, ((0, 0), (0, 1)), k), xf, mf, emit_to(x4.at[k]))
-        last_send(k).start()
+        level(mats(mt, ((0, 0), (0, 1)), k), xf, mf, emit_to(x4.at[k]), None, lambda: last_send(k, 0).start())
+        last_send(k, 1).start()
 
     def fourth_own(k):
         await_pair(k, lambda q: mat_copy(7, q).wait())
@@ -283,7 +298,8 @@
 
     def fourth_level(k):
         await_pair(k, lambda q: mat_copy(8, q).wait())
-        last_send(k).wait_recv()
+        last_send(k, 0).wait_recv()
+        last_send(k, 1).wait_recv()
         fill(0, x4p.at[k])
         half = lax.rem(tile(k), 2)
         level(mats(mt, ((1, 1),), k), xf, mf, keep(fin.at[half]), part.at[k])
@@ -309,24 +325,33 @@
 
     def step(n, _):
         for late, stage in stages:
-
-            @pl.when(jnp.logical_and(n >= late, n < TILES + late))
-            def _(late=late, stage=stage):
-                stage(n - late)
+            joined = late > LAGS[2]
+
+            @pl.when(jnp.logical_and(n >= late, n < TILES + late - joined))
+            def _(late=late, stage=stage, joined=joined):
+                def run(k, _):
+                    stage(k)
+                    return 0
+
+                k = n - late
+                lax.fori_loop(k, jnp.where(k == 6, 8, k + 1) if joined else k + 1, run, 0)
 
         return 0
 
-    lax.fori_loop(0, TILES + stages[-1][0], step, 0)
+    lax.fori_loop(0, TILES + max(LAGS) - 1, step, 0)
 
     def finish(k):
-        far_send(k).wait_send()
+        far_send(k, 0).wait_send()
+        far_send(k, 1).wait_send()
         for d in (1, 2, 3):
             y_send(k, d).wait_send()
-        last_send(k).wait_send()
+        last_send(k, 0).wait_send()
+        last_send(k, 1).wait_send()
 
         @pl.when(k > 0)
         def _():
-            swap_send(k).wait_send()
+            swap_send(k, 0).wait_send()
+            swap_send(k, 1).wait_send()
 
     def finish_pair(q):
         coeff_send(q).wait_send()
@@ -363,9 +388,9 @@
             pltpu.VMEM((2, 2, 4, 32, 128), F32),
             pltpu.VMEM((8, 32, 8, 128), F32),
             pltpu.VMEM((2, 32, 8, 128), F32),
-            dma(9, 4), dma(4), dma(4), dma(4), dma(8), dma(8), dma(8), dma(8),
+            dma(9, 4), dma(4), dma(4), dma(4), dma(8, 2), dma(8, 2), dma(8, 2), dma(8, 2),
             pltpu.SemaphoreType.DMA,
-            dma(8, 4), dma(8, 4), dma(8), dma(8), dma(8), dma(4),
+            dma(8, 4), dma(8, 4), dma(8), dma(8, 2), dma(8, 2), dma(4),
         ],
         compiler_params=pltpu.CompilerParams(
             collective_id=0, has_side_effects=True, vmem_limit_bytes=60 << 20

time: 49.4 us -> 48.3 us (0.978)
  Pallas kernels: 47.3 us -> 46.3 us
    pallas_call x1, Pallas kernels: 47.3 us -> 46.3 us  [per_device(): pl.pallas_call(kernel, out_shape=jax.ShapeDtypeStruct((32, 64, 128), BF16...]
where the time goes in v1:
time: 48.3 us; the launch traced here: 48.2 us
  Pallas kernels  46.3 us (96%)
  local copies, waits for them, and re-layouts  1.87 us (4%)
    pallas_call x1, Pallas kernels, per_device(): pl.pallas_call(kernel, out_shape=jax.ShapeDtypeStruct((32, 64, 128), BF16...  46.3 us
    unnamed x1, local copies, waits for them, and re-layouts  1.87 us

profile of v1, /device:TPU:0, one launch (start us, length us, event | category | flops | bytes accessed | tf_op | source)
XLA Modules:
  0.0 48.2 jit_solution(2468890926049084765)
XLA Ops:
  0.0 46.3 %butterfly.1 = bf16[32,64,128]{2,1,0:T(8,128)(2,1)} custom-call(bf16[32,64,128]{2,1,0:T(8,128)(2,1)} %bitcast.11, bf16[2,2,32,32,1024]{4,3,2,1,0:T(8,128)(2,1)} %source.1, bf16[32,32,1024]{2,1,0:T(8,128)(2,1)} %middle.1, bf16[2,2,32,32,1024]{4,3,2,1,0:T(8,128)(2,1)} %target.1), custom_call_target="tpu_custom_call" | custom-call | tf_op jit(solution)/shard_map/butterfly/pallas_call | solution.py:368
  46.3 1.9 %copy.6 = bf16[32,8,1024]{2,1,0:T(8,128)(2,1)} copy(bf16[32,8,1024]{2,1,0:T(8,128)(2,1)} %bitcast.10) | data formatting | bytes 1048576
